TPU v7x, 256 devices: a whole 4x4x8 slice. The times are simulated.
256 devices in a mesh: samp: 32 (over y_hi, z, core), par: 8 (over y_lo, x).
Axes of the slice: x: 4, y: 4 (y_hi: 2, y_lo: 2; y = y_hi * 2 + y_lo), z: 8, core: 2. Of those that a mesh axis runs over, the one named last changes fastest.
Arguments:
- jacobian: float32 [256, 65536], P('samp', 'par'), may hold values from -32 to 32
- energies: float32 [256], P('samp'), may hold values from -20 to 24
Outputs:
- update: float32 [65536], P('par')
- coeffs: float32 [256], P('samp')
All inputs are finite; a program needn't handle non-finite values.
Results may differ from a plain program's by a relative error of at most 0.0029.
Values may be sent and summed in bfloat16 or wider, within the bound.
A program may use at most 64 MiB of HBM per device.

v0:
```python
import math

import jax
import jax.numpy as jnp
from jax import lax
from jax.sharding import PartitionSpec as P

P_SIZE = 65536
ITERS = 3


diag_shift = 0.05


def squares(residual):
    return lax.psum(jnp.sum(residual * residual), "samp")


def per_device(jacobian, energies):
    local_rows = jacobian.shape[0]
    sample_count = local_rows * lax.axis_size("samp")
    column_sums, energy_total = lax.psum((jnp.sum(jacobian, axis=0), jnp.sum(energies)), "samp")
    mean_col = column_sums / sample_count
    scaled = ((jacobian - mean_col[None, :]) / math.sqrt(P_SIZE)).astype(jnp.bfloat16)
    right_side = energy_total / sample_count - energies
    partial_rows = lax.dot_general(
        scaled,
        lax.all_gather(scaled, "samp", axis=0, tiled=True),
        (((1,), (1,)), ((), ())),
        preferred_element_type=jnp.float32,
    )
    gram_rows = lax.psum(partial_rows, "par")
    coeffs = jnp.zeros_like(right_side)
    residual = right_side
    direction = right_side
    norm_now = squares(residual)
    for turn_index in range(ITERS):
        whole_vector = lax.all_gather(direction, "samp", axis=0, tiled=True)
        product = jnp.dot(
            gram_rows,
            whole_vector,
            precision=lax.Precision.HIGHEST,
            preferred_element_type=jnp.float32,
        )
        image = product + diag_shift * direction
        curvature = lax.psum(jnp.sum(direction * image), "samp")
        step_size = norm_now / curvature
        coeffs = coeffs + step_size * direction
        residual = residual - step_size * image
        norm_next = squares(residual)
        direction = residual + norm_next / norm_now * direction
        norm_now = norm_next
    update_part = jnp.dot(
        coeffs, scaled, precision=lax.Precision.HIGHEST, preferred_element_type=jnp.float32
    )
    update = lax.psum(update_part, "samp")
    return (update, coeffs)


def solution(mesh):
    return jax.shard_map(
        per_device,
        mesh=mesh,
        in_specs=(P("samp", "par"), P("samp")),
        out_specs=(P("par"), P("samp")),
        check_vma=False,
    )
```

profile of v0, /device:TPU:1, one launch (start us, length us, event | category | flops | bytes accessed | tf_op | source)
XLA Modules:
  0.0 919.7 jit_solution(1024457080413128686)
XLA Ops:
  7.2 0.0 all-gather.2.cloned.1.call-start
  7.2 1.3 reduce_sum.72
  8.5 69.7 %psum.70 = f32[]{:T(128)} all-reduce(f32[]{:T(128)} %reduce_sum.72), channel_id=1, replica_groups=mesh['samp'=32,'par'=8] {'samp'}, use_global_device_ids=true, to_apply=%region_1.0 | all-reduce | flops 1 | bytes 8 | tf_op jit(solution)/shard_map/psum | solution.py:22
  78.2 1.3 dynamic-slice
  80.8 1.0 reduce_sum.74
  81.8 0.8 fusion.9
  82.6 127.8 %all-reduce.4 = (f32[8192]{0:T(1024)S(1)}, f32[256]{0:T(256)S(1)}) all-reduce(f32[8192]{0:T(1024)S(1)} %reduce_sum.74, f32[256]{0:T(256)S(1)} %get-tuple-element.14), channel_id=1, replica_groups=mesh['samp'=32,'par'=8] {'samp'}, use_global_device_ids=true, to_apply=%region_5.0 | all-reduce | flops 8448 | bytes 67584 | tf_op jit(solution)/shard_map/psum | solution.py:22
  210.4 1.6 multiply_convert_fusion
  212.0 0.0 copy-start
  212.0 0.0 all-gather.2.cloned.1.call-update
  212.1 86.9 %all-gather.2.cloned.1.call-done = bf16[256,8192]{1,0:T(8,128)(2,1)} async-done(((bf16[8,8192]{1,0:T(8,128)(2,1)}), bf16[256,8192]{1,0:T(8,128)(2,1)}) %all-gather.2.cloned.1.call-update) | async-done | bytes 4194320 | tf_op jit(solution)/shard_map/all_gather | solution.py:28
  299.0 3.4 fusion.10
  302.5 15.2 %psum.73 = f32[8,256]{1,0:T(8,128)S(1)} all-reduce(f32[8,256]{1,0:T(8,128)S(1)} %fusion.10), channel_id=1, replica_groups=mesh['samp'=32,'par'=8] {'par'}, use_global_device_ids=true, to_apply=%region_6.0 | all-reduce | flops 2048 | bytes 16384 | tf_op jit(solution)/shard_map/psum | solution.py:32
  317.6 0.8 multiply_reduce_fusion.3
  318.4 69.0 %all-reduce.3 = (f32[]{:T(128)}, f32[]{:T(128)}) all-reduce(f32[]{:T(128)} %get-tuple-element.3, f32[]{:T(128)} %get-tuple-element.2), channel_id=1, replica_groups=mesh['samp'=32,'par'=8] {'samp'}, use_global_device_ids=true, to_apply=%region_3.0 | all-reduce | flops 2 | bytes 16 | tf_op jit(solution)/shard_map/psum | solution.py:16
  388.7 0.6 multiply_reduce_fusion.2
  389.3 65.6 %psum.75 = f32[]{:T(128)} all-reduce(f32[]{:T(128)} %get-tuple-element.12), channel_id=1, replica_groups=mesh['samp'=32,'par'=8] {'samp'}, use_global_device_ids=true, to_apply=%region_10.0 | all-reduce | flops 1 | bytes 8 | tf_op jit(solution)/shard_map/psum | solution.py:16
  456.2 0.1 fusion.8
  456.3 65.0 %all-reduce.1 = f32[256]{0:T(256)S(1)} all-reduce(f32[256]{0:T(256)S(1)} %get-tuple-element.10), channel_id=1, replica_groups=mesh['samp'=32,'par'=8] {'samp'}, use_global_device_ids=true, to_apply=%add.1 | all-reduce | flops 256 | bytes 2048
  521.3 0.8 multiply_reduce_fusion.1
  522.1 65.5 %psum.76 = f32[]{:T(128)} all-reduce(f32[]{:T(128)} %get-tuple-element.17), channel_id=1, replica_groups=mesh['samp'=32,'par'=8] {'samp'}, use_global_device_ids=true, to_apply=%region_12.0 | all-reduce | flops 1 | bytes 8 | tf_op jit(solution)/shard_map/psum | solution.py:46
  588.9 0.7 multiply_reduce_fusion
  589.6 65.6 %psum.77 = f32[]{:T(128)} all-reduce(f32[]{:T(128)} %multiply_reduce_fusion), channel_id=1, replica_groups=mesh['samp'=32,'par'=8] {'samp'}, use_global_device_ids=true, to_apply=%region_14.0 | all-reduce | flops 1 | bytes 8 | tf_op jit(solution)/shard_map/psum | solution.py:16
  656.6 0.1 fusion.7
  656.7 65.0 %all-reduce.2 = f32[256]{0:T(256)S(1)} all-reduce(f32[256]{0:T(256)S(1)} %get-tuple-element.8), channel_id=1, replica_groups=mesh['samp'=32,'par'=8] {'samp'}, use_global_device_ids=true, to_apply=%add.2 | all-reduce | flops 256 | bytes 2048
  721.7 0.7 fusion.4
  722.4 65.6 %psum.78 = f32[]{:T(128)} all-reduce(f32[]{:T(128)} %fusion.4), channel_id=1, replica_groups=mesh['samp'=32,'par'=8] {'samp'}, use_global_device_ids=true, to_apply=%region_16.0 | all-reduce | flops 1 | bytes 8 | tf_op jit(solution)/shard_map/psum | solution.py:46
  789.4 0.0 copy-done
  789.5 0.0 copy-start.1
  789.5 0.3 fusion.5
  789.7 123.2 %psum.79 = f32[8192]{0:T(1024)} all-reduce(f32[8192]{0:T(1024)S(1)} %bitcast.33), channel_id=1, replica_groups=mesh['samp'=32,'par'=8] {'samp'}, use_global_device_ids=true, to_apply=%region_17.0 | all-reduce | flops 8192 | bytes 65536 | tf_op jit(solution)/shard_map/psum | solution.py:56
  912.9 0.0 copy-done.1
  (5 shorter events, 0.0 us)
Async XLA Ops:
  7.2 291.9 %all-gather.2.cloned.1.call-start = ((), (), s32[]{:S(2)}) async-start(), calls=%async_computation | async-start | bytes 4325376 | tf_op jit(solution)/shard_map/all_gather | solution.py:28
  212.0 577.4 %copy-start = (bf16[8,8192]{1,0:T(8,128)(2,1)S(1)}, bf16[8,8192]{1,0:T(8,128)(2,1)}, u32[]{:S(2)}) copy-start(bf16[8,8192]{1,0:T(8,128)(2,1)} %multiply_convert_fusion) | copy-start | bytes 393220
  789.5 123.5 %copy-start.1 = (f32[8]{0:T(128)}, f32[8]{0:T(128)S(1)}, u32[]{:S(2)}) copy-start(f32[8]{0:T(128)S(1)} %multiply_add_fusion) | copy-start | bytes 100
Sparse Core Ops, SparseCore 0:
  212.2 86.7 all-gather.1
where the time goes:
time: 925 us; the launch traced here: 920 us
  blocking collectives  797 us (86%)
  waiting for transfers between devices  87 us (9%)
  between operations  21.9 us (2%)
    psum x3, blocking collectives, squares(): return lax.psum(jnp.sum(residual * residual), 'samp')  200 us
    psum x2, blocking collectives, per_device(): lax.psum((jnp.sum(jacobian, axis=0), jnp.sum(energies)), 'samp')  198 us
    psum x2, blocking collectives, per_device(): curvature = lax.psum(jnp.sum(direction * image), 'samp')  131 us
    unnamed x2, blocking collectives  130 us
    psum x1, blocking collectives, per_device(): update = lax.psum(update_part, 'samp')  123 us
    all_gather x1, waiting for transfers between devices, per_device(): lax.all_gather(scaled, 'samp', axis=0, tiled=True)  86.9 us
  transfers between devices with their start and end apart: 1, of which 1 were waited for; matrix products, arithmetic and copies ran while one was open for 0% of the time, Pallas kernels for 0%

commit v1 on v0

v1 whole, which is shorter than its diff:
```python
import functools

import jax
import jax.numpy as jnp
from jax import lax
from jax.experimental import pallas as pl
from jax.experimental.pallas import tpu as pltpu
from jax.sharding import PartitionSpec as P

P_SIZE = 65536
ITERS = 3
SHIFT = 0.05
CORES = 2
Y_HI = 2
LANES = 128
MESH = pl.DeviceIdType.MESH


def total_rows(block):
    return jnp.sum(block, axis=0, keepdims=True)


def total_lanes(block):
    return jnp.sum(block, axis=1, keepdims=True)


def kernel(
    samp,
    par,
    jac,
    energies,
    update,
    coeffs,
    jbuf,
    ebuf,
    eown,
    scaled_ref,
    gpart,
    rs,
    ar,
    gram,
    upiece,
    send,
    recv,
):
    depth = samp // (CORES * Y_HI)
    plane = CORES * Y_HI * par
    rows, width = jbuf.shape[1], jbuf.shape[2]
    count = samp * rows

    s = lax.axis_index("samp")
    p = lax.axis_index("par")
    core = lax.rem(s, CORES)
    z = lax.rem(s // CORES, depth)
    y_hi = s // (CORES * depth)
    a = (y_hi * par + p) * CORES + core

    def samp_peer(k):
        return lax.rem(s + k, samp), p

    def plane_peer(k):
        there = lax.rem(a + k, plane)
        there_core = lax.rem(there, CORES)
        there_p = lax.rem(there // CORES, par)
        there_y = there // (CORES * par)
        return there, ((there_y * depth + z) * CORES + there_core, there_p)

    def depth_peer(k):
        there = lax.rem(z + k, depth)
        return (y_hi * depth + there) * CORES + core, p

    def each(first, last, body):
        def step(k, carry):
            body(k)
            return carry

        lax.fori_loop(first, last, step, 0)

    def remote(src, dst, which, device):
        return pltpu.make_async_remote_copy(
            src_ref=src,
            dst_ref=dst,
            send_sem=send.at[which],
            recv_sem=recv.at[which],
            device_id=device,
            device_id_type=MESH,
        )

    def landed(block, which):
        pltpu.make_async_copy(block, block, recv.at[which]).wait()

    def sent(block, which):
        pltpu.make_async_copy(block, block, send.at[which]).wait()

    barrier = pltpu.get_barrier_semaphore()

    def greet(device):
        pl.semaphore_signal(barrier, inc=1, device_id=device, device_id_type=MESH)

    each(1, samp, lambda k: greet(samp_peer(k)))

    def greet_plane(k):
        there_p = lax.rem(p + 1 + k // (CORES * Y_HI), par)
        rest = lax.rem(k, CORES * Y_HI)
        there_s = ((rest // CORES) * depth + z) * CORES + lax.rem(rest, CORES)
        greet((there_s, there_p))

    each(0, CORES * Y_HI * (par - 1), greet_plane)

    own = pltpu.make_async_copy(
        jac.at[:, pl.ds(pl.multiple_of(s * width, width), width)], jbuf.at[s], recv.at[0]
    )
    own.start()
    lane = lax.broadcasted_iota(jnp.int32, (1, LANES), 1)
    offset = lax.rem(s * rows, LANES)
    mine = jnp.zeros((1, LANES), jnp.float32)
    for r in range(rows):
        mine = jnp.where(lane == offset + r, energies[r], mine)
    eown[...] = mine
    ebuf[s] = mine

    pl.semaphore_wait(barrier, samp - 1 + CORES * Y_HI * (par - 1))

    def exchange(k):
        there, there_p = samp_peer(k)
        remote(
            jac.at[:, pl.ds(pl.multiple_of(there * width, width), width)],
            jbuf.at[s],
            0,
            (there, there_p),
        ).start()

    each(1, samp, exchange)
    each(1, samp, lambda k: remote(eown, ebuf.at[s], 1, samp_peer(k)).start())

    landed(jbuf, 0)
    block = jbuf[...].reshape(count, width)
    mean_col = total_rows(block) / count
    scaled = ((block - mean_col) * (1.0 / P_SIZE**0.5)).astype(jnp.bfloat16)
    scaled_ref[...] = scaled
    part = lax.dot_general(
        scaled, scaled, (((1,), (1,)), ((), ())), preferred_element_type=jnp.float32
    )
    gpart[...] = part.reshape(gpart.shape)

    def scatter(k):
        there, device = plane_peer(k)
        remote(gpart.at[there], rs.at[a], 2, device).start()

    each(1, plane, scatter)
    rs[a] = gpart[a]

    landed(ebuf.at[pl.ds(0, samp - 1)], 1)
    per = LANES // rows
    level = jnp.concatenate(
        [jnp.sum(ebuf[i * per : (i + 1) * per], axis=0) for i in range(samp // per)], axis=1
    )
    right_row = total_lanes(level) / count - level
    diagonal = lax.broadcasted_iota(jnp.int32, (count, count), 0) == lax.broadcasted_iota(
        jnp.int32, (count, count), 1
    )
    right_col = total_lanes(jnp.where(diagonal, right_row, 0.0))

    landed(rs.at[pl.ds(0, plane - 1)], 2)
    ar[z] = jnp.sum(rs[...], axis=0)
    each(1, depth, lambda k: remote(ar.at[z], ar.at[z], 3, depth_peer(k)).start())
    landed(ar.at[pl.ds(0, depth - 1)], 3)
    gram[a] = jnp.sum(ar[...], axis=0)
    each(1, plane, lambda k: remote(gram.at[a], gram.at[a], 4, plane_peer(k)[1]).start())
    landed(gram.at[pl.ds(0, plane - 1)], 4)

    g = gram[...].reshape(count, count)
    d_row, d_col = right_row, right_col
    r_row, r_col = right_row, right_col
    c_row, c_col = jnp.zeros_like(right_row), jnp.zeros_like(right_col)
    rr = total_lanes(r_row * r_row)
    for turn in range(ITERS):
        image_row = total_rows(g * d_col) + SHIFT * d_row
        size = rr / total_lanes(d_row * image_row)
        c_row = c_row + size * d_row
        c_col = c_col + size * d_col
        if turn == ITERS - 1:
            break
        image_col = total_lanes(g * d_row) + SHIFT * d_col
        r_row = r_row - size * image_row
        r_col = r_col - size * image_col
        fresh = total_lanes(r_row * r_row)
        ratio = fresh / rr
        d_row = r_row + ratio * d_row
        d_col = r_col + ratio * d_col
        rr = fresh

    upiece[s] = total_rows(scaled_ref[...].astype(jnp.float32) * c_col)
    each(1, samp, lambda k: remote(upiece.at[s], upiece.at[s], 5, samp_peer(k)).start())

    here = s // per
    half = c_row[:, :LANES]
    for i in range(1, samp // per):
        half = jnp.where(here == i, c_row[:, i * LANES : (i + 1) * LANES], half)
    coeffs[...] = pltpu.roll(half, lax.rem(LANES - offset, LANES), 1)

    sent(jbuf.at[pl.ds(0, samp - 1)], 0)
    sent(ebuf.at[pl.ds(0, samp - 1)], 1)
    sent(rs.at[pl.ds(0, plane - 1)], 2)
    sent(ar.at[pl.ds(0, depth - 1)], 3)
    sent(gram.at[pl.ds(0, plane - 1)], 4)
    landed(upiece.at[pl.ds(0, samp - 1)], 5)
    update[...] = upiece[...]
    sent(upiece.at[pl.ds(0, samp - 1)], 5)


def solution(mesh):
    samp, par = mesh.shape["samp"], mesh.shape["par"]
    plane = CORES * Y_HI * par
    depth = samp // (CORES * Y_HI)

    def per_device(jacobian, energies):
        rows, columns = jacobian.shape
        width = columns // samp
        count = rows * samp
        update, coeffs = pl.pallas_call(
            functools.partial(kernel, samp, par),
            out_shape=(
                jax.ShapeDtypeStruct((samp, 1, width), jnp.float32),
                jax.ShapeDtypeStruct((1, LANES), jnp.float32),
            ),
            in_specs=[
                pl.BlockSpec(memory_space=pl.ANY),
                pl.BlockSpec(memory_space=pltpu.SMEM),
            ],
            out_specs=(
                pl.BlockSpec(memory_space=pltpu.VMEM),
                pl.BlockSpec(memory_space=pltpu.VMEM),
            ),
            scratch_shapes=[
                pltpu.VMEM((samp, rows, width), jnp.float32),
                pltpu.VMEM((samp, 1, LANES), jnp.float32),
                pltpu.VMEM((1, LANES), jnp.float32),
                pltpu.VMEM((count, width), jnp.bfloat16),
                pltpu.VMEM((plane, count // plane, count), jnp.float32),
                pltpu.VMEM((plane, count // plane, count), jnp.float32),
                pltpu.VMEM((depth, count // plane, count), jnp.float32),
                pltpu.VMEM((plane, count // plane, count), jnp.float32),
                pltpu.VMEM((samp, 1, width), jnp.float32),
                pltpu.SemaphoreType.DMA((6,)),
                pltpu.SemaphoreType.DMA((6,)),
            ],
            compiler_params=pltpu.CompilerParams(collective_id=0, has_side_effects=True),
        )(jacobian, energies)
        return update.reshape(columns), coeffs[0, :rows]

    return jax.shard_map(
        per_device,
        mesh=mesh,
        in_specs=(P("samp", "par"), P("samp")),
        out_specs=(P("par"), P("samp")),
        check_vma=False,
    )
```

time: 925 us -> 49.8 us (0.05)
  blocking collectives: 797 us -> 0 us
  waiting for transfers between devices: 87 us -> 0 us
  Pallas kernels: 0 us -> 46.4 us
  between operations: 21.9 us -> 0.65 us
    psum x9 -> x0, blocking collectives: 667 us -> none  [the longest x3 200 us: squares(): return lax.psum(jnp.sum(residual * residual), 'samp')]
    unnamed x2 -> x0, blocking collectives: 130 us -> none
    all_gather x1 -> x0, waiting for transfers between devices: 86.9 us -> none  [per_device(): lax.all_gather(scaled, 'samp', axis=0, tiled=True)]
    pallas_call x0 -> x1, Pallas kernels: none -> 46.4 us  [per_device(): pl.pallas_call(functools.partial(kernel, samp, par), out_shape=(jax.Shape...]
  transfers between devices with their start and end apart: 1 -> 0, of which waited for: 1 -> 0; matrix products, arithmetic and copies ran while one was open for 0% -> 0% of each run, Pallas kernels for 0% -> 0%
where the time goes in v1:
time: 49.8 us; the launch traced here: 49.6 us
  Pallas kernels  46.4 us (93%)
  local copies, waits for them, and re-layouts  2.51 us (5%)
  between operations  0.65 us (1%)
    pallas_call x1, Pallas kernels, per_device(): pl.pallas_call(functools.partial(kernel, samp, par), out_shape=(jax.Shape...  46.4 us
    unnamed x3, local copies, waits for them, and re-layouts  2 us

profile of v1, /device:TPU:1, one launch (start us, length us, event | category | flops | bytes accessed | tf_op | source)
XLA Modules:
  0.0 49.6 jit_solution(7188958413421368896)
XLA Ops:
  0.6 46.4 %shard_map.41 = (f32[32,1,256]{2,1,0:T(1,128)}, f32[1,128]{1,0:T(1,128)}) custom-call(f32[8,8192]{1,0:T(8,128)} %jac.1, f32[8]{0:T(128)} %energies.1), custom_call_target="tpu_custom_call" | custom-call | tf_op jit(solution)/shard_map/pallas_call | solution.py:221
  47.1 0.0 copy-start
  47.1 0.6 %copy-done = f32[1,128]{1,0:T(1,128)S(1)} copy-done((f32[1,128]{1,0:T(1,128)S(1)}, f32[1,128]{1,0:T(1,128)}, u32[]{:S(2)}) %copy-start) | copy-done | bytes 536
  47.7 0.5 %slice_bitcast_fusion = f32[8]{0:T(128)} fusion(f32[1,128]{1,0:T(1,128)S(1)} %copy-done), kind=kLoop, calls=%fused_computation | loop fusion | bytes 64 | tf_op jit(solution)/shard_map/squeeze | solution.py:250
  48.2 1.4 %copy.5 = f32[8192]{0:T(1024)} copy(f32[8192]{0:T(1024)} %bitcast.3) | data formatting | bytes 65536
Async XLA Ops:
  47.1 0.6 %copy-start = (f32[1,128]{1,0:T(1,128)S(1)}, f32[1,128]{1,0:T(1,128)}, u32[]{:S(2)}) copy-start(f32[1,128]{1,0:T(1,128)} %get-tuple-element.5) | copy-start | bytes 1540

commit v2 on v1

v2 whole, which is shorter than its diff:
```python
import functools

import jax
import jax.numpy as jnp
from jax import lax
from jax.experimental import pallas as pl
from jax.experimental.pallas import tpu as pltpu
from jax.sharding import PartitionSpec as P

P_SIZE = 65536
ITERS = 3
SHIFT = 0.05
CORES = 2
Y_HI = 2
Y_LO = 2
LANES = 128
VMEM_BYTES = 8 * 2**20
MESH = pl.DeviceIdType.MESH


def total_rows(block):
    return jnp.sum(block, axis=0, keepdims=True)


def total_lanes(block):
    return jnp.sum(block, axis=1, keepdims=True)


def each(count, body):
    def step(k, carry):
        body(k)
        return carry

    lax.fori_loop(0, count, step, 0)


def kernel(
    samp,
    par,
    jac,
    energies,
    out,
    jbuf,
    ebuf,
    eown,
    scaled_ref,
    gpart,
    rs,
    ar,
    top,
    low,
    upiece,
    send,
    recv,
):
    depth = samp // (CORES * Y_HI)
    xs = par // Y_LO
    ys = Y_HI * Y_LO
    chips = xs * ys
    rows, width = jbuf.shape[1], jbuf.shape[2]
    count = samp * rows
    half = count // 2
    per = LANES // rows

    s = lax.axis_index("samp")
    p = lax.axis_index("par")
    core = lax.rem(s, CORES)
    z = lax.rem(s // CORES, depth)
    y_hi = s // (CORES * depth)
    x = lax.rem(p, xs)
    y = y_hi * Y_LO + p // xs
    chip = y * xs + x
    rank = core * chips + chip
    right = pl.ds(half, half)

    def samp_at(there_z, y_off, core_off):
        there_y = lax.rem(y_hi + y_off, Y_HI)
        return (there_y * depth + there_z) * CORES + lax.rem(core + core_off, CORES)

    z_steps = sorted(range(depth), key=lambda k: -min(k, depth - k))

    def samp_peers(body):
        for z_off in z_steps:
            there_z = lax.rem(z + z_off, depth)

            def step(k):
                body(samp_at(there_z, lax.rem(k // CORES + 1, Y_HI), k + 1))

            each(CORES * Y_HI - (1 if z_off == 0 else 0), step)

    def ring(n):
        return lax.rem(2 + n * (7 - n) // 2, 4)

    def plane_chip(k):
        there_y = lax.rem(y + ring(k // xs), ys)
        return there_y, lax.rem(x + ring(lax.rem(k, xs)), xs)

    def on_chip(there_y, there_x, there_core):
        there_s = ((there_y // Y_LO) * depth + z) * CORES + there_core
        return there_s, lax.rem(there_y, Y_LO) * xs + there_x

    def remote(src, dst, which, device):
        return pltpu.make_async_remote_copy(
            src_ref=src,
            dst_ref=dst,
            send_sem=send.at[which],
            recv_sem=recv.at[which],
            device_id=device,
            device_id_type=MESH,
        )

    def landed(block, which):
        pltpu.make_async_copy(block, block, recv.at[which]).wait()

    def sent(block, which):
        pltpu.make_async_copy(block, block, send.at[which]).wait()

    def columns(there):
        return jac.at[:, pl.ds(pl.multiple_of(there * width, width), width)]

    barrier = pltpu.get_barrier_semaphore()

    def greet(device):
        pl.semaphore_signal(barrier, inc=1, device_id=device, device_id_type=MESH)

    samp_peers(lambda there: greet((there, p)))
    each(par - 1, lambda k: greet((s, lax.rem(p + 1 + k, par))))

    own = pltpu.make_async_copy(columns(s), jbuf.at[s], recv.at[0])
    own.start()
    lane = lax.broadcasted_iota(jnp.int32, (1, LANES), 1)
    offset = lax.rem(s * rows, LANES)
    mine = jnp.zeros((1, LANES), jnp.float32)
    for r in range(rows):
        mine = jnp.where(lane == offset + r, energies[r], mine)
    eown[...] = mine
    ebuf[s] = mine

    pl.semaphore_wait(barrier, samp - 1 + par - 1)

    samp_peers(lambda there: remote(columns(there), jbuf.at[s], 0, (there, p)).start())
    samp_peers(lambda there: remote(eown, ebuf.at[s], 1, (there, p)).start())

    landed(jbuf, 0)
    block = jbuf[...].reshape(count, width)
    mean_col = total_rows(block) / count
    scaled = ((block - mean_col) * (1.0 / P_SIZE**0.5)).astype(jnp.bfloat16)
    scaled_ref[...] = scaled
    part = lax.dot_general(
        scaled, scaled, (((1,), (1,)), ((), ())), preferred_element_type=jnp.float32
    )
    gpart[...] = part.reshape(gpart.shape)

    def scatter(k):
        there_y, there_x = plane_chip(k)
        there = there_y * xs + there_x
        remote(gpart.at[there], rs.at[rank], 2, on_chip(there_y, there_x, 0)).start()
        remote(
            gpart.at[chips + there, :, right],
            rs.at[rank, :, right],
            2,
            on_chip(there_y, there_x, 1),
        ).start()

    each(chips - 1, scatter)

    @pl.when(core == 0)
    def _():
        remote(gpart.at[chips + chip, :, right], rs.at[rank, :, right], 2, on_chip(y, x, 1)).start()

    @pl.when(core == 1)
    def _():
        remote(gpart.at[chip], rs.at[rank], 2, on_chip(y, x, 0)).start()

    rs[rank] = gpart[rank]

    landed(ebuf.at[pl.ds(0, samp - 1)], 1)
    level = jnp.concatenate(
        [jnp.sum(ebuf[i * per : (i + 1) * per], axis=0) for i in range(samp // per)], axis=1
    )
    right_row = total_lanes(level) / count - level
    diagonal = lax.broadcasted_iota(jnp.int32, (count, count), 0) == lax.broadcasted_iota(
        jnp.int32, (count, count), 1
    )
    right_col = total_lanes(jnp.where(diagonal, right_row, 0.0))

    others = pl.ds(0, 2 * chips - 1)
    z_others = pl.ds(0, depth - 1)

    def reduce_rows(part_of, mine_of, which):
        landed(rs.at[others, :, part_of], 2)
        ar[z, :, part_of] = jnp.sum(rs[:, :, part_of], axis=0)
        for k in z_steps[:-1]:
            remote(
                ar.at[z, :, part_of],
                ar.at[z, :, part_of],
                3,
                (samp_at(lax.rem(z + k, depth), 0, 0), p),
            ).start()
        landed(ar.at[z_others, :, part_of], 3)
        mine_of[chip] = jnp.sum(ar[:, :, part_of], axis=0)

        def spread(k):
            there_y, there_x = plane_chip(k)
            for there_core in range(CORES):
                remote(
                    mine_of.at[chip], mine_of.at[chip], which, on_chip(there_y, there_x, there_core)
                ).start()

        each(chips - 1, spread)
        remote(mine_of.at[chip], mine_of.at[chip], which, on_chip(y, x, 1 - core)).start()

    @pl.when(core == 0)
    def _():
        reduce_rows(pl.ds(0, count), top, 4)
        landed(top.at[pl.ds(0, chips - 1)], 4)
        landed(low, 5)

    @pl.when(core == 1)
    def _():
        reduce_rows(right, low, 5)
        landed(top, 4)
        landed(low.at[pl.ds(0, chips - 1)], 5)

    upper = top[...].reshape(half, count)
    lower = jnp.concatenate([jnp.transpose(upper[:, half:]), low[...].reshape(half, half)], axis=1)
    g = jnp.concatenate([upper, lower], axis=0)
    d_row, d_col = right_row, right_col
    r_row, r_col = right_row, right_col
    c_row, c_col = jnp.zeros_like(right_row), jnp.zeros_like(right_col)
    rr = total_lanes(r_row * r_row)
    for turn in range(ITERS):
        image_row = total_rows(g * d_col) + SHIFT * d_row
        size = rr / total_lanes(d_row * image_row)
        c_row = c_row + size * d_row
        c_col = c_col + size * d_col
        if turn == ITERS - 1:
            break
        image_col = total_lanes(g * d_row) + SHIFT * d_col
        r_row = r_row - size * image_row
        r_col = r_col - size * image_col
        fresh = total_lanes(r_row * r_row)
        ratio = fresh / rr
        d_row = r_row + ratio * d_row
        d_col = r_col + ratio * d_col
        rr = fresh

    upiece[s] = total_rows(scaled_ref[...].astype(jnp.float32) * c_col)
    samp_peers(lambda there: remote(upiece.at[s], upiece.at[s], 6, (there, p)).start())

    here = s // per
    piece = c_row[:, :LANES]
    for i in range(1, samp // per):
        piece = jnp.where(here == i, c_row[:, i * LANES : (i + 1) * LANES], piece)
    out[samp] = jnp.concatenate(
        [pltpu.roll(piece, lax.rem(LANES - offset, LANES), 1)] * (width // LANES), axis=1
    )

    sent(jbuf.at[pl.ds(0, samp - 1)], 0)
    sent(ebuf.at[pl.ds(0, samp - 1)], 1)

    @pl.when(core == 0)
    def _():
        sent(gpart.at[pl.ds(0, chips - 1)], 2)
        sent(gpart.at[pl.ds(0, chips), :, right], 2)
        sent(ar.at[z_others], 3)
        sent(rs.at[others], 4)

    @pl.when(core == 1)
    def _():
        sent(gpart.at[pl.ds(0, chips)], 2)
        sent(gpart.at[pl.ds(0, chips - 1), :, right], 2)
        sent(ar.at[z_others, :, right], 3)
        sent(rs.at[others, :, right], 5)

    landed(upiece.at[pl.ds(0, samp - 1)], 6)
    out[0:samp] = upiece[...]
    sent(upiece.at[pl.ds(0, samp - 1)], 6)


def solution(mesh):
    samp, par = mesh.shape["samp"], mesh.shape["par"]
    chips = Y_HI * par
    depth = samp // (CORES * Y_HI)

    def per_device(jacobian, energies):
        rows, columns = jacobian.shape
        width = columns // samp
        count = rows * samp
        half = count // 2
        share = half // chips
        out = pl.pallas_call(
            functools.partial(kernel, samp, par),
            out_shape=jax.ShapeDtypeStruct((samp + 1, 1, width), jnp.float32),
            in_specs=[
                pl.BlockSpec(memory_space=pl.ANY),
                pl.BlockSpec(memory_space=pltpu.SMEM),
            ],
            out_specs=pl.BlockSpec(memory_space=pltpu.VMEM),
            scratch_shapes=[
                pltpu.VMEM((samp, rows, width), jnp.float32),
                pltpu.VMEM((samp, 1, LANES), jnp.float32),
                pltpu.VMEM((1, LANES), jnp.float32),
                pltpu.VMEM((count, width), jnp.bfloat16),
                pltpu.VMEM((2 * chips, share, count), jnp.float32),
                pltpu.VMEM((2 * chips, share, count), jnp.float32),
                pltpu.VMEM((depth, share, count), jnp.float32),
                pltpu.VMEM((chips, share, count), jnp.float32),
                pltpu.VMEM((chips, share, half), jnp.float32),
                pltpu.VMEM((samp, 1, width), jnp.float32),
                pltpu.SemaphoreType.DMA((7,)),
                pltpu.SemaphoreType.DMA((7,)),
            ],
            compiler_params=pltpu.CompilerParams(
                collective_id=0, has_side_effects=True, vmem_limit_bytes=VMEM_BYTES
            ),
        )(
            pltpu.with_memory_space_constraint(jacobian, pltpu.HBM),
            pltpu.with_memory_space_constraint(energies, pltpu.HBM),
        )
        return out[:samp].reshape(columns), out[samp, 0, :rows]

    return jax.shard_map(
        per_device,
        mesh=mesh,
        in_specs=(P("samp", "par"), P("samp")),
        out_specs=(P("par"), P("samp")),
        check_vma=False,
    )
```

time: 49.8 us -> 44.5 us (0.89)
  Pallas kernels: 46.4 us -> 42.6 us
  local copies, waits for them, and re-layouts: 2.51 us -> 1.13 us
    pallas_call x1, Pallas kernels: 46.4 us -> 42.6 us  [per_device(): pl.pallas_call(functools.partial(kernel, samp, par), out_shape=jax.ShapeD...]
    unnamed x3 -> x0, local copies, waits for them, and re-layouts: 2 us -> none
    slice x0 -> x1, local copies, waits for them, and re-layouts: none -> 0.62 us  [per_device(): return (out[:samp].reshape(columns), out[samp, 0, :rows])]
where the time goes in v2:
time: 44.5 us; the launch traced here: 44.4 us
  Pallas kernels  42.6 us (96%)
  local copies, waits for them, and re-layouts  1.13 us (3%)
  between operations  0.64 us (1%)
    pallas_call x1, Pallas kernels, per_device(): pl.pallas_call(functools.partial(kernel, samp, par), out_shape=jax.ShapeD...  42.6 us

profile of v2, /device:TPU:1, one launch (start us, length us, event | category | flops | bytes accessed | tf_op | source)
XLA Modules:
  0.0 44.4 jit_solution(1686994942605254168)
XLA Ops:
  0.6 42.6 %shard_map.41 = f32[33,1,256]{2,1,0:T(1,128)S(1)} custom-call(f32[8,8192]{1,0:T(8,128)} %jac.1, f32[8]{0:T(128)} %energies.1), custom_call_target="tpu_custom_call" | custom-call | tf_op jit(solution)/shard_map/pallas_call | solution.py:292
  43.3 0.5 %slice_bitcast_fusion = f32[8]{0:T(128)} fusion(f32[33,1,256]{2,1,0:T(1,128)S(1)} %shard_map.41), kind=kLoop, calls=%fused_computation | loop fusion | bytes 64 | tf_op jit(solution)/shard_map/squeeze | solution.py:321
  43.8 0.6 %slice.6 = f32[32,1,256]{2,1,0:T(1,128)} slice(f32[33,1,256]{2,1,0:T(1,128)S(1)} %shard_map.41), slice={[0:32], [0:1], [0:256]} | slice | bytes 65536 | tf_op jit(solution)/shard_map/slice | solution.py:321

commit v3 on v2

--- a/solution.py
+++ b/solution.py
@@ -39,7 +39,10 @@
     par,
     jac,
     energies,
-    out,
+    update,
+    coeffs,
+    jown,
+    elist,
     jbuf,
     ebuf,
     eown,
@@ -52,6 +55,7 @@
     upiece,
     send,
     recv,
+    local,
 ):
     depth = samp // (CORES * Y_HI)
     xs = par // Y_LO
@@ -126,22 +130,27 @@
     samp_peers(lambda there: greet((there, p)))
     each(par - 1, lambda k: greet((s, lax.rem(p + 1 + k, par))))
 
-    own = pltpu.make_async_copy(columns(s), jbuf.at[s], recv.at[0])
-    own.start()
+    def stage(there):
+        pltpu.make_async_copy(columns(there), jown.at[there], local.at[0]).start()
+
+    each(samp, stage)
+    level_copy = pltpu.make_async_copy(energies, elist, local.at[1])
+    level_copy.start()
+    level_copy.wait()
     lane = lax.broadcasted_iota(jnp.int32, (1, LANES), 1)
     offset = lax.rem(s * rows, LANES)
     mine = jnp.zeros((1, LANES), jnp.float32)
     for r in range(rows):
-        mine = jnp.where(lane == offset + r, energies[r], mine)
+        mine = jnp.where(lane == offset + r, elist[r], mine)
     eown[...] = mine
     ebuf[s] = mine
+    pltpu.make_async_copy(jown, jown, local.at[0]).wait()
+    jbuf[s] = jown[s]
 
     pl.semaphore_wait(barrier, samp - 1 + par - 1)
 
-    samp_peers(lambda there: remote(columns(there), jbuf.at[s], 0, (there, p)).start())
-    samp_peers(lambda there: remote(eown, ebuf.at[s], 1, (there, p)).start())
-
-    landed(jbuf, 0)
+    samp_peers(lambda there: remote(jown.at[there], jbuf.at[s], 0, (there, p)).start())
+    landed(jbuf.at[pl.ds(0, samp - 1)], 0)
     block = jbuf[...].reshape(count, width)
     mean_col = total_rows(block) / count
     scaled = ((block - mean_col) * (1.0 / P_SIZE**0.5)).astype(jnp.bfloat16)
@@ -174,6 +183,46 @@
 
     rs[rank] = gpart[rank]
 
+    samp_peers(lambda there: remote(eown, ebuf.at[s], 1, (there, p)).start())
+
+    others = pl.ds(0, 2 * chips - 1)
+    z_others = pl.ds(0, depth - 1)
+
+    every = pl.ds(0, count)
+
+    def across_z(part_of):
+        landed(rs.at[others, :, part_of], 2)
+        ar[z, :, part_of] = jnp.sum(rs[:, :, part_of], axis=0)
+        for k in z_steps[:-1]:
+            remote(
+                ar.at[z, :, part_of],
+                ar.at[z, :, part_of],
+                3,
+                (samp_at(lax.rem(z + k, depth), 0, 0), p),
+            ).start()
+
+    def spread(part_of, mine_of, which):
+        landed(ar.at[z_others, :, part_of], 3)
+        mine_of[chip] = jnp.sum(ar[:, :, part_of], axis=0)
+
+        def step(k):
+            there_y, there_x = plane_chip(k)
+            for there_core in range(CORES):
+                remote(
+                    mine_of.at[chip], mine_of.at[chip], which, on_chip(there_y, there_x, there_core)
+                ).start()
+
+        each(chips - 1, step)
+        remote(mine_of.at[chip], mine_of.at[chip], which, on_chip(y, x, 1 - core)).start()
+
+    @pl.when(core == 0)
+    def _():
+        across_z(every)
+
+    @pl.when(core == 1)
+    def _():
+        across_z(right)
+
     landed(ebuf.at[pl.ds(0, samp - 1)], 1)
     level = jnp.concatenate(
         [jnp.sum(ebuf[i * per : (i + 1) * per], axis=0) for i in range(samp // per)], axis=1
@@ -184,41 +233,15 @@
     )
     right_col = total_lanes(jnp.where(diagonal, right_row, 0.0))
 
-    others = pl.ds(0, 2 * chips - 1)
-    z_others = pl.ds(0, depth - 1)
-
-    def reduce_rows(part_of, mine_of, which):
-        landed(rs.at[others, :, part_of], 2)
-        ar[z, :, part_of] = jnp.sum(rs[:, :, part_of], axis=0)
-        for k in z_steps[:-1]:
-            remote(
-                ar.at[z, :, part_of],
-                ar.at[z, :, part_of],
-                3,
-                (samp_at(lax.rem(z + k, depth), 0, 0), p),
-            ).start()
-        landed(ar.at[z_others, :, part_of], 3)
-        mine_of[chip] = jnp.sum(ar[:, :, part_of], axis=0)
-
-        def spread(k):
-            there_y, there_x = plane_chip(k)
-            for there_core in range(CORES):
-                remote(
-                    mine_of.at[chip], mine_of.at[chip], which, on_chip(there_y, there_x, there_core)
-                ).start()
-
-        each(chips - 1, spread)
-        remote(mine_of.at[chip], mine_of.at[chip], which, on_chip(y, x, 1 - core)).start()
-
     @pl.when(core == 0)
     def _():
-        reduce_rows(pl.ds(0, count), top, 4)
+        spread(every, top, 4)
         landed(top.at[pl.ds(0, chips - 1)], 4)
         landed(low, 5)
 
     @pl.when(core == 1)
     def _():
-        reduce_rows(right, low, 5)
+        spread(right, low, 5)
         landed(top, 4)
         landed(low.at[pl.ds(0, chips - 1)], 5)
 
@@ -252,9 +275,7 @@
     piece = c_row[:, :LANES]
     for i in range(1, samp // per):
         piece = jnp.where(here == i, c_row[:, i * LANES : (i + 1) * LANES], piece)
-    out[samp] = jnp.concatenate(
-        [pltpu.roll(piece, lax.rem(LANES - offset, LANES), 1)] * (width // LANES), axis=1
-    )
+    coeffs[...] = pltpu.roll(piece, lax.rem(LANES - offset, LANES), 1)[0, :rows]
 
     sent(jbuf.at[pl.ds(0, samp - 1)], 0)
     sent(ebuf.at[pl.ds(0, samp - 1)], 1)
@@ -274,8 +295,32 @@
         sent(rs.at[others, :, right], 5)
 
     landed(upiece.at[pl.ds(0, samp - 1)], 6)
-    out[0:samp] = upiece[...]
+    update[...] = upiece[...]
     sent(upiece.at[pl.ds(0, samp - 1)], 6)
+
+
+def hand_over_kernel(update, coeffs, update_out, coeffs_out, done):
+    first = pltpu.make_async_copy(update, update_out, done.at[0])
+    second = pltpu.make_async_copy(coeffs, coeffs_out, done.at[1])
+    first.start()
+    second.start()
+    first.wait()
+    second.wait()
+
+
+def hand_over(update, coeffs):
+    anywhere = pl.BlockSpec(memory_space=pl.ANY)
+    return pl.pallas_call(
+        hand_over_kernel,
+        out_shape=(
+            jax.ShapeDtypeStruct(update.shape, update.dtype),
+            jax.ShapeDtypeStruct(coeffs.shape, coeffs.dtype),
+        ),
+        in_specs=[anywhere, anywhere],
+        out_specs=(anywhere, anywhere),
+        scratch_shapes=[pltpu.SemaphoreType.DMA((2,))],
+        compiler_params=pltpu.CompilerParams(vmem_limit_bytes=VMEM_BYTES),
+    )(update, coeffs)
 
 
 def solution(mesh):
@@ -289,15 +334,23 @@
         count = rows * samp
         half = count // 2
         share = half // chips
-        out = pl.pallas_call(
+        update, coeffs = pl.pallas_call(
             functools.partial(kernel, samp, par),
-            out_shape=jax.ShapeDtypeStruct((samp + 1, 1, width), jnp.float32),
+            out_shape=(
+                jax.ShapeDtypeStruct((samp, 1, width), jnp.float32),
+                jax.ShapeDtypeStruct((rows,), jnp.float32),
+            ),
             in_specs=[
                 pl.BlockSpec(memory_space=pl.ANY),
-                pl.BlockSpec(memory_space=pltpu.SMEM),
+                pl.BlockSpec(memory_space=pl.ANY),
             ],
-            out_specs=pl.BlockSpec(memory_space=pltpu.VMEM),
+            out_specs=(
+                pl.BlockSpec(memory_space=pltpu.VMEM),
+                pl.BlockSpec(memory_space=pltpu.VMEM),
+            ),
             scratch_shapes=[
+                pltpu.VMEM((samp, rows, width), jnp.float32),
+                pltpu.SMEM((rows,), jnp.float32),
                 pltpu.VMEM((samp, rows, width), jnp.float32),
                 pltpu.VMEM((samp, 1, LANES), jnp.float32),
                 pltpu.VMEM((1, LANES), jnp.float32),
@@ -310,6 +363,7 @@
                 pltpu.VMEM((samp, 1, width), jnp.float32),
                 pltpu.SemaphoreType.DMA((7,)),
                 pltpu.SemaphoreType.DMA((7,)),
+                pltpu.SemaphoreType.DMA((2,)),
             ],
             compiler_params=pltpu.CompilerParams(
                 collective_id=0, has_side_effects=True, vmem_limit_bytes=VMEM_BYTES
@@ -318,7 +372,7 @@
             pltpu.with_memory_space_constraint(jacobian, pltpu.HBM),
             pltpu.with_memory_space_constraint(energies, pltpu.HBM),
         )
-        return out[:samp].reshape(columns), out[samp, 0, :rows]
+        return hand_over(update.reshape(columns), coeffs)
 
     return jax.shard_map(
         per_device,

time: 44.5 us -> 43 us (0.966)
  local copies, waits for them, and re-layouts: 1.13 us -> 0 us
    slice x1 -> x0, local copies, waits for them, and re-layouts: 0.62 us -> none  [per_device(): return (out[:samp].reshape(columns), out[samp, 0, :rows])]
    squeeze x1 -> x0, local copies, waits for them, and re-layouts: 0.51 us -> none  [per_device(): return (out[:samp].reshape(columns), out[samp, 0, :rows])]
    pallas_call x1 -> x2, Pallas kernels: 42.6 us -> 42.3 us  [the longest x1 41.6 us: per_device(): pl.pallas_call(functools.partial(kernel, samp, par), out_shape=(jax.Shape...]
where the time goes in v3:
time: 43 us; the launch traced here: 42.9 us
  Pallas kernels  42.3 us (98%)
  between operations  0.64 us (1%)
    pallas_call x1, Pallas kernels, per_device(): pl.pallas_call(functools.partial(kernel, samp, par), out_shape=(jax.Shape...  41.6 us

profile of v3, /device:TPU:1, one launch (start us, length us, event | category | flops | bytes accessed | tf_op | source)
XLA Modules:
  0.0 42.9 jit_solution(1812251437294566355)
XLA Ops:
  0.6 41.6 %shard_map.41 = (f32[32,1,256]{2,1,0:T(1,128)S(1)}, f32[8]{0:T(128)S(1)}) custom-call(f32[8,8192]{1,0:T(8,128)} %jac.1, f32[8]{0:T(128)} %energies.1), custom_call_target="tpu_custom_call" | custom-call | tf_op jit(solution)/shard_map/pallas_call | solution.py:337
  42.3 0.6 %shard_map.42 = (f32[8192]{0:T(1024)}, f32[8]{0:T(128)}) custom-call(f32[8192]{0:T(1024)S(1)} %bitcast.1, f32[8]{0:T(128)S(1)} %get-tuple-element.5.coeffs), custom_call_target="tpu_custom_call" | custom-call | tf_op jit(solution)/shard_map/pallas_call | solution.py:313

commit v4 on v3

--- a/solution.py
+++ b/solution.py
@@ -52,7 +52,6 @@
     ar,
     top,
     low,
-    upiece,
     send,
     recv,
     local,
@@ -77,31 +76,39 @@
     rank = core * chips + chip
     right = pl.ds(half, half)
 
-    def samp_at(there_z, y_off, core_off):
-        there_y = lax.rem(y_hi + y_off, Y_HI)
-        return (there_y * depth + there_z) * CORES + lax.rem(core + core_off, CORES)
-
-    z_steps = sorted(range(depth), key=lambda k: -min(k, depth - k))
+    def away(step, size):
+        return min(step, size - step)
+
+    y_at = [lax.rem(y + k, ys) for k in range(ys)]
+    x_at = [lax.rem(x + k, xs) for k in range(xs)]
+    z_at = [lax.rem(z + k, depth) for k in range(depth)]
+    y_hi_at = [lax.rem(y_hi + k, Y_HI) for k in range(Y_HI)]
+    core_at = [core, 1 - core]
+    plane_s = [((there // Y_LO) * depth + z) * CORES for there in y_at]
+    plane_p = [lax.rem(there, Y_LO) * xs for there in y_at]
+    z_steps = sorted(range(1, depth), key=lambda k: -away(k, depth))
+    chip_steps = sorted(
+        [(j, i) for j in range(ys) for i in range(xs) if (j, i) != (0, 0)],
+        key=lambda k: -away(k[0], ys) - away(k[1], xs),
+    )
+    samp_steps = sorted(
+        [(j, k, c) for j in range(Y_HI) for k in range(depth) for c in range(CORES) if j + k + c],
+        key=lambda k: (-2 * k[0] - away(k[1], depth), -k[2]),
+    )
+    samp_ids = [(y_hi_at[j] * depth + z_at[k]) * CORES + core_at[c] for j, k, c in samp_steps]
+    z_ids = [(y_hi * depth + z_at[k]) * CORES + core for k in z_steps]
 
     def samp_peers(body):
-        for z_off in z_steps:
-            there_z = lax.rem(z + z_off, depth)
-
-            def step(k):
-                body(samp_at(there_z, lax.rem(k // CORES + 1, Y_HI), k + 1))
-
-            each(CORES * Y_HI - (1 if z_off == 0 else 0), step)
-
-    def ring(n):
-        return lax.rem(2 + n * (7 - n) // 2, 4)
-
-    def plane_chip(k):
-        there_y = lax.rem(y + ring(k // xs), ys)
-        return there_y, lax.rem(x + ring(lax.rem(k, xs)), xs)
-
-    def on_chip(there_y, there_x, there_core):
-        there_s = ((there_y // Y_LO) * depth + z) * CORES + there_core
-        return there_s, lax.rem(there_y, Y_LO) * xs + there_x
+        for there in samp_ids:
+            body(there)
+
+    def on_chip(step, there_core):
+        return plane_s[step[0]] + there_core, plane_p[step[0]] + x_at[step[1]]
+
+    def chip_of(step):
+        return y_at[step[0]] * xs + x_at[step[1]]
+
+    here_chip = (0, 0)
 
     def remote(src, dst, which, device):
         return pltpu.make_async_remote_copy(
@@ -161,25 +168,25 @@
     gpart[...] = part.reshape(gpart.shape)
 
     def scatter(k):
-        there_y, there_x = plane_chip(k)
-        there = there_y * xs + there_x
-        remote(gpart.at[there], rs.at[rank], 2, on_chip(there_y, there_x, 0)).start()
+        there = chip_of(k)
+        remote(gpart.at[there], rs.at[rank], 2, on_chip(k, 0)).start()
         remote(
             gpart.at[chips + there, :, right],
             rs.at[rank, :, right],
             2,
-            on_chip(there_y, there_x, 1),
+            on_chip(k, 1),
         ).start()
 
-    each(chips - 1, scatter)
+    for k in chip_steps:
+        scatter(k)
 
     @pl.when(core == 0)
     def _():
-        remote(gpart.at[chips + chip, :, right], rs.at[rank, :, right], 2, on_chip(y, x, 1)).start()
+        remote(gpart.at[chips + chip, :, right], rs.at[rank, :, right], 2, on_chip(here_chip, 1)).start()
 
     @pl.when(core == 1)
     def _():
-        remote(gpart.at[chip], rs.at[rank], 2, on_chip(y, x, 0)).start()
+        remote(gpart.at[chip], rs.at[rank], 2, on_chip(here_chip, 0)).start()
 
     rs[rank] = gpart[rank]
 
@@ -193,12 +200,12 @@
     def across_z(part_of):
         landed(rs.at[others, :, part_of], 2)
         ar[z, :, part_of] = jnp.sum(rs[:, :, part_of], axis=0)
-        for k in z_steps[:-1]:
+        for there in z_ids:
             remote(
                 ar.at[z, :, part_of],
                 ar.at[z, :, part_of],
                 3,
-                (samp_at(lax.rem(z + k, depth), 0, 0), p),
+                (there, p),
             ).start()
 
     def spread(part_of, mine_of, which):
@@ -206,14 +213,14 @@
         mine_of[chip] = jnp.sum(ar[:, :, part_of], axis=0)
 
         def step(k):
-            there_y, there_x = plane_chip(k)
             for there_core in range(CORES):
                 remote(
-                    mine_of.at[chip], mine_of.at[chip], which, on_chip(there_y, there_x, there_core)
+                    mine_of.at[chip], mine_of.at[chip], which, on_chip(k, there_core)
                 ).start()
 
-        each(chips - 1, step)
-        remote(mine_of.at[chip], mine_of.at[chip], which, on_chip(y, x, 1 - core)).start()
+        for k in chip_steps:
+            step(k)
+        remote(mine_of.at[chip], mine_of.at[chip], which, on_chip(here_chip, 1 - core)).start()
 
     @pl.when(core == 0)
     def _():
@@ -268,8 +275,8 @@
         d_col = r_col + ratio * d_col
         rr = fresh
 
-    upiece[s] = total_rows(scaled_ref[...].astype(jnp.float32) * c_col)
-    samp_peers(lambda there: remote(upiece.at[s], upiece.at[s], 6, (there, p)).start())
+    update[s] = total_rows(scaled_ref[...].astype(jnp.float32) * c_col)
+    samp_peers(lambda there: remote(update.at[s], update.at[s], 6, (there, p)).start())
 
     here = s // per
     piece = c_row[:, :LANES]
@@ -294,9 +301,8 @@
         sent(ar.at[z_others, :, right], 3)
         sent(rs.at[others, :, right], 5)
 
-    landed(upiece.at[pl.ds(0, samp - 1)], 6)
-    update[...] = upiece[...]
-    sent(upiece.at[pl.ds(0, samp - 1)], 6)
+    sent(update.at[pl.ds(0, samp - 1)], 6)
+    landed(update.at[pl.ds(0, samp - 1)], 6)
 
 
 def hand_over_kernel(update, coeffs, update_out, coeffs_out, done):
@@ -360,7 +366,6 @@
                 pltpu.VMEM((depth, share, count), jnp.float32),
                 pltpu.VMEM((chips, share, count), jnp.float32),
                 pltpu.VMEM((chips, share, half), jnp.float32),
-                pltpu.VMEM((samp, 1, width), jnp.float32),
                 pltpu.SemaphoreType.DMA((7,)),
                 pltpu.SemaphoreType.DMA((7,)),
                 pltpu.SemaphoreType.DMA((2,)),

time: 43 us -> 42.4 us (0.986)
  Pallas kernels: 42.3 us -> 41.6 us
    pallas_call x1, Pallas kernels: 41.6 us -> 41 us  [per_device(): pl.pallas_call(functools.partial(kernel, samp, par), out_shape=(jax.Shape...]
where the time goes in v4:
time: 42.4 us; the launch traced here: 42.3 us
  Pallas kernels  41.6 us (98%)
  between operations  0.64 us (2%)
    pallas_call x1, Pallas kernels, per_device(): pl.pallas_call(functools.partial(kernel, samp, par), out_shape=(jax.Shape...  41 us

profile of v4, /device:TPU:1, one launch (start us, length us, event | category | flops | bytes accessed | tf_op | source)
XLA Modules:
  0.0 42.3 jit_solution(1204402292925745959)
XLA Ops:
  0.6 41.0 %shard_map.41 = (f32[32,1,256]{2,1,0:T(1,128)S(1)}, f32[8]{0:T(128)S(1)}) custom-call(f32[8,8192]{1,0:T(8,128)} %jac.1, f32[8]{0:T(128)} %energies.1), custom_call_target="tpu_custom_call" | custom-call | tf_op jit(solution)/shard_map/pallas_call | solution.py:343
  41.6 0.6 %shard_map.42 = (f32[8192]{0:T(1024)}, f32[8]{0:T(128)}) custom-call(f32[8192]{0:T(1024)S(1)} %bitcast.1, f32[8]{0:T(128)S(1)} %get-tuple-element.5.coeffs), custom_call_target="tpu_custom_call" | custom-call | tf_op jit(solution)/shard_map/pallas_call | solution.py:319

commit v5 on v4

v5 whole, which is shorter than its diff:
```python
import functools

import jax
import jax.numpy as jnp
from jax import lax
from jax.experimental import pallas as pl
from jax.experimental.pallas import tpu as pltpu
from jax.sharding import PartitionSpec as P

P_SIZE = 65536
ITERS = 3
SHIFT = 0.05
CORES = 2
Y_HI = 2
Y_LO = 2
LANES = 128
VMEM_BYTES = 8 * 2**20
MESH = pl.DeviceIdType.MESH


def total_rows(block):
    return jnp.sum(block, axis=0, keepdims=True)


def total_lanes(block):
    return jnp.sum(block, axis=1, keepdims=True)


def each(count, body):
    def step(k, carry):
        body(k)
        return carry

    lax.fori_loop(0, count, step, 0)


def kernel(
    samp,
    par,
    jac,
    energies,
    update,
    coeffs,
    jown,
    elist,
    jbuf,
    ebuf,
    eown,
    scaled_ref,
    gpart,
    rs,
    ar,
    top,
    low,
    cown,
    cbuf,
    send,
    recv,
    local,
):
    depth = samp // (CORES * Y_HI)
    team = samp // Y_HI
    xs = par // Y_LO
    chips = par
    rows, width = jbuf.shape[1], jbuf.shape[2]
    count = samp * rows
    half = count // 2
    per = LANES // rows

    s = lax.axis_index("samp")
    p = lax.axis_index("par")
    core = lax.rem(s, CORES)
    z = lax.rem(s // CORES, depth)
    x = lax.rem(p, xs)
    y = p // xs
    rank = core * chips + p
    right = pl.ds(half, half)
    worker = s < team
    sender = jnp.logical_not(worker)

    def away(step, size):
        return min(step, size - step)

    x_at = [lax.rem(x + k, xs) for k in range(xs)]
    y_at = [y, 1 - y]
    z_at = [lax.rem(z + k, depth) for k in range(depth)]
    core_at = [core, 1 - core]
    z_steps = sorted(range(depth), key=lambda k: -away(k, depth))
    z_ids = [z_at[k] * CORES + core for k in z_steps[:-1]]
    team_ids = [z_at[k] * CORES + core_at[c] for k in z_steps for c in (1, 0)]
    chip_steps = sorted(
        [(j, i) for j in range(Y_LO) for i in range(xs) if (j, i) != (0, 0)],
        key=lambda k: -k[0] - away(k[1], xs),
    )
    chip_ids = [y_at[j] * xs + x_at[i] for j, i in chip_steps]

    def at_core(there_core):
        return z * CORES + there_core

    def remote(src, dst, which, device):
        return pltpu.make_async_remote_copy(
            src_ref=src,
            dst_ref=dst,
            send_sem=send.at[which],
            recv_sem=recv.at[which],
            device_id=device,
            device_id_type=MESH,
        )

    def landed(block, which):
        pltpu.make_async_copy(block, block, recv.at[which]).wait()

    def sent(block, which):
        pltpu.make_async_copy(block, block, send.at[which]).wait()

    def columns(there):
        return jac.at[:, pl.ds(pl.multiple_of(there * width, width), width)]

    barrier = pltpu.get_barrier_semaphore()

    def greet(device):
        pl.semaphore_signal(barrier, inc=1, device_id=device, device_id_type=MESH)

    @pl.when(worker)
    def _():
        for there in team_ids:
            greet((there + team, p))
        for there in team_ids[:-1]:
            greet((there, p))
        each(par - 1, lambda k: greet((s, lax.rem(p + 1 + k, par))))

    def stage(there):
        pltpu.make_async_copy(columns(there), jown.at[there], local.at[0]).start()

    each(team, stage)
    level_copy = pltpu.make_async_copy(energies, elist, local.at[1])
    level_copy.start()
    level_copy.wait()
    lane = lax.broadcasted_iota(jnp.int32, (1, LANES), 1)
    offset = lax.rem(s * rows, LANES)
    mine = jnp.zeros((1, LANES), jnp.float32)
    for r in range(rows):
        mine = jnp.where(lane == offset + r, elist[r], mine)
    eown[...] = mine
    pltpu.make_async_copy(jown, jown, local.at[0]).wait()

    def give_rows(there):
        remote(jown.at[there], jbuf.at[s], 0, (there, p)).start()

    def give_energies(there):
        remote(eown, ebuf.at[s], 1, (there, p)).start()

    def work():
        block = jbuf[...].reshape(count, width)
        mean_col = total_rows(block) / count
        scaled = ((block - mean_col) * (1.0 / P_SIZE**0.5)).astype(jnp.bfloat16)
        scaled_ref[...] = scaled
        part = lax.dot_general(
            scaled, scaled, (((1,), (1,)), ((), ())), preferred_element_type=jnp.float32
        )
        gpart[...] = part.reshape(gpart.shape)

        def scatter(there):
            remote(gpart.at[there], rs.at[rank], 2, (at_core(0), there)).start()
            remote(
                gpart.at[chips + there, :, right], rs.at[rank, :, right], 2, (at_core(1), there)
            ).start()

        for there in chip_ids:
            scatter(there)

        @pl.when(core == 0)
        def _():
            remote(gpart.at[chips + p, :, right], rs.at[rank, :, right], 2, (at_core(1), p)).start()

        @pl.when(core == 1)
        def _():
            remote(gpart.at[p], rs.at[rank], 2, (at_core(0), p)).start()

        rs[rank] = gpart[rank]
        for there in team_ids[:-1]:
            give_energies(there)

        others = pl.ds(0, 2 * chips - 1)
        z_others = pl.ds(0, depth - 1)
        every = pl.ds(0, count)

        def across_z(part_of):
            landed(rs.at[others, :, part_of], 2)
            ar[z, :, part_of] = jnp.sum(rs[:, :, part_of], axis=0)
            for there in z_ids:
                remote(ar.at[z, :, part_of], ar.at[z, :, part_of], 3, (there, p)).start()

        def spread(part_of, mine_of, which):
            landed(ar.at[z_others, :, part_of], 3)
            mine_of[p] = jnp.sum(ar[:, :, part_of], axis=0)
            for there in chip_ids:
                for there_core in range(CORES):
                    remote(mine_of.at[p], mine_of.at[p], which, (at_core(there_core), there)).start()
            remote(mine_of.at[p], mine_of.at[p], which, (at_core(1 - core), p)).start()

        @pl.when(core == 0)
        def _():
            across_z(every)

        @pl.when(core == 1)
        def _():
            across_z(right)

        landed(ebuf.at[pl.ds(0, samp - 1)], 1)
        level = jnp.concatenate(
            [jnp.sum(ebuf[i * per : (i + 1) * per], axis=0) for i in range(samp // per)], axis=1
        )
        right_row = total_lanes(level) / count - level
        diagonal = lax.broadcasted_iota(jnp.int32, (count, count), 0) == lax.broadcasted_iota(
            jnp.int32, (count, count), 1
        )
        right_col = total_lanes(jnp.where(diagonal, right_row, 0.0))

        @pl.when(core == 0)
        def _():
            spread(every, top, 4)
            landed(top.at[pl.ds(0, chips - 1)], 4)
            landed(low, 5)

        @pl.when(core == 1)
        def _():
            spread(right, low, 5)
            landed(top, 4)
            landed(low.at[pl.ds(0, chips - 1)], 5)

        above = top[...].reshape(half, count)
        below = jnp.concatenate([jnp.transpose(above[:, half:]), low[...].reshape(half, half)], axis=1)
        g = jnp.concatenate([above, below], axis=0)
        d_row, d_col = right_row, right_col
        r_row, r_col = right_row, right_col
        c_row, c_col = jnp.zeros_like(right_row), jnp.zeros_like(right_col)
        rr = total_lanes(r_row * r_row)
        for turn in range(ITERS):
            image_row = total_rows(g * d_col) + SHIFT * d_row
            size = rr / total_lanes(d_row * image_row)
            c_row = c_row + size * d_row
            c_col = c_col + size * d_col
            if turn == ITERS - 1:
                break
            image_col = total_lanes(g * d_row) + SHIFT * d_col
            r_row = r_row - size * image_row
            r_col = r_col - size * image_col
            fresh = total_lanes(r_row * r_row)
            ratio = fresh / rr
            d_row = r_row + ratio * d_row
            d_col = r_col + ratio * d_col
            rr = fresh

        update[s] = total_rows(scaled_ref[...].astype(jnp.float32) * c_col)

        def give_piece(there):
            remote(update.at[s], update.at[s], 6, (there, p)).start()

        for there in team_ids[:-1]:
            give_piece(there)
            give_piece(there + team)
        give_piece(s + team)

        def own_samples(first):
            here = lax.rem(s, team) // per
            piece = c_row[:, first : first + LANES]
            for i in range(1, team // per):
                piece = jnp.where(here == i, c_row[:, first + i * LANES : first + (i + 1) * LANES], piece)
            return pltpu.roll(piece, lax.rem(LANES - offset, LANES), 1)

        cown[...] = own_samples(half)
        remote(cown, cbuf, 7, (s + team, p)).start()
        coeffs[...] = own_samples(0)[0, :rows]

        sent(jbuf.at[pl.ds(0, team - 1)], 0)
        sent(ebuf.at[pl.ds(0, team - 1)], 1)

        @pl.when(core == 0)
        def _():
            sent(gpart.at[pl.ds(0, chips - 1)], 2)
            sent(gpart.at[pl.ds(0, chips), :, right], 2)
            sent(ar.at[z_others], 3)
            sent(rs.at[others], 4)

        @pl.when(core == 1)
        def _():
            sent(gpart.at[pl.ds(0, chips)], 2)
            sent(gpart.at[pl.ds(0, chips - 1), :, right], 2)
            sent(ar.at[z_others, :, right], 3)
            sent(rs.at[others, :, right], 5)

        sent(update, 6)
        sent(update.at[pl.ds(0, team - 1)], 6)
        sent(cown, 7)
        landed(update.at[pl.ds(0, team - 1)], 6)


    @pl.when(sender)
    def _():
        pl.semaphore_wait(barrier, team)
        for there in team_ids:
            give_rows(there)
        for there in team_ids:
            give_energies(there)
        landed(cbuf, 7)
        coeffs[...] = cbuf[...][0, :rows]
        sent(jbuf.at[pl.ds(0, team)], 0)
        sent(ebuf.at[pl.ds(0, team)], 1)
        landed(update, 6)

    @pl.when(worker)
    def _():
        pl.semaphore_wait(barrier, team - 1 + par - 1)
        for there in team_ids[:-1]:
            give_rows(there)
        ebuf[s] = mine
        jbuf[s] = jown[s]
        landed(jbuf.at[pl.ds(0, samp - 1)], 0)
        work()


def hand_over_kernel(update, coeffs, update_out, coeffs_out, done):
    first = pltpu.make_async_copy(update, update_out, done.at[0])
    second = pltpu.make_async_copy(coeffs, coeffs_out, done.at[1])
    first.start()
    second.start()
    first.wait()
    second.wait()


def hand_over(update, coeffs):
    anywhere = pl.BlockSpec(memory_space=pl.ANY)
    return pl.pallas_call(
        hand_over_kernel,
        out_shape=(
            jax.ShapeDtypeStruct(update.shape, update.dtype),
            jax.ShapeDtypeStruct(coeffs.shape, coeffs.dtype),
        ),
        in_specs=[anywhere, anywhere],
        out_specs=(anywhere, anywhere),
        scratch_shapes=[pltpu.SemaphoreType.DMA((2,))],
        compiler_params=pltpu.CompilerParams(vmem_limit_bytes=VMEM_BYTES),
    )(update, coeffs)


def solution(mesh):
    samp, par = mesh.shape["samp"], mesh.shape["par"]
    chips = par
    depth = samp // (CORES * Y_HI)
    team = samp // Y_HI

    def per_device(jacobian, energies):
        rows, columns = jacobian.shape
        width = columns // team
        count = rows * samp
        half = count // 2
        share = half // chips
        update, coeffs = pl.pallas_call(
            functools.partial(kernel, samp, par),
            out_shape=(
                jax.ShapeDtypeStruct((team, 1, width), jnp.float32),
                jax.ShapeDtypeStruct((rows,), jnp.float32),
            ),
            in_specs=[
                pl.BlockSpec(memory_space=pl.ANY),
                pl.BlockSpec(memory_space=pl.ANY),
            ],
            out_specs=(
                pl.BlockSpec(memory_space=pltpu.VMEM),
                pl.BlockSpec(memory_space=pltpu.VMEM),
            ),
            scratch_shapes=[
                pltpu.VMEM((team, rows, width), jnp.float32),
                pltpu.SMEM((rows,), jnp.float32),
                pltpu.VMEM((samp, rows, width), jnp.float32),
                pltpu.VMEM((samp, 1, LANES), jnp.float32),
                pltpu.VMEM((1, LANES), jnp.float32),
                pltpu.VMEM((count, width), jnp.bfloat16),
                pltpu.VMEM((2 * chips, share, count), jnp.float32),
                pltpu.VMEM((2 * chips, share, count), jnp.float32),
                pltpu.VMEM((depth, share, count), jnp.float32),
                pltpu.VMEM((chips, share, count), jnp.float32),
                pltpu.VMEM((chips, share, half), jnp.float32),
                pltpu.VMEM((1, LANES), jnp.float32),
                pltpu.VMEM((1, LANES), jnp.float32),
                pltpu.SemaphoreType.DMA((8,)),
                pltpu.SemaphoreType.DMA((8,)),
                pltpu.SemaphoreType.DMA((2,)),
            ],
            compiler_params=pltpu.CompilerParams(
                collective_id=0, has_side_effects=True, vmem_limit_bytes=VMEM_BYTES
            ),
        )(
            pltpu.with_memory_space_constraint(jacobian, pltpu.HBM),
            pltpu.with_memory_space_constraint(energies, pltpu.HBM),
        )
        return hand_over(update.reshape(columns), coeffs)

    return jax.shard_map(
        per_device,
        mesh=mesh,
        in_specs=(P("samp", "par"), P("samp")),
        out_specs=(P("par"), P("samp")),
        check_vma=False,
    )
```

time: 42.4 us -> 41.1 us (0.969)
  Pallas kernels: 41.6 us -> 40.3 us
    pallas_call x1, Pallas kernels: 41 us -> 39.7 us  [per_device(): pl.pallas_call(functools.partial(kernel, samp, par), out_shape=(jax.Shape...]
where the time goes in v5:
time: 41.1 us; the launch traced here: 40.9 us
  Pallas kernels  40.3 us (98%)
  between operations  0.64 us (2%)
    pallas_call x1, Pallas kernels, per_device(): pl.pallas_call(functools.partial(kernel, samp, par), out_shape=(jax.Shape...  39.7 us

profile of v5, /device:TPU:1, one launch (start us, length us, event | category | flops | bytes accessed | tf_op | source)
XLA Modules:
  0.0 40.9 jit_solution(15480065007662606452)
XLA Ops:
  0.6 39.7 %shard_map.41 = (f32[16,1,512]{2,1,0:T(1,128)S(1)}, f32[8]{0:T(128)S(1)}) custom-call(f32[8,8192]{1,0:T(8,128)} %jac.1, f32[8]{0:T(128)} %energies.1), custom_call_target="tpu_custom_call" | custom-call | tf_op jit(solution)/shard_map/pallas_call | solution.py:359
  40.3 0.6 %shard_map.42 = (f32[8192]{0:T(1024)}, f32[8]{0:T(128)}) custom-call(f32[8192]{0:T(1024)S(1)} %bitcast.1, f32[8]{0:T(128)S(1)} %get-tuple-element.5.coeffs), custom_call_target="tpu_custom_call" | custom-call | tf_op jit(solution)/shard_map/pallas_call | solution.py:334

commit v6 on v5

--- a/solution.py
+++ b/solution.py
@@ -154,7 +154,7 @@
         block = jbuf[...].reshape(count, width)
         mean_col = total_rows(block) / count
         scaled = ((block - mean_col) * (1.0 / P_SIZE**0.5)).astype(jnp.bfloat16)
-        scaled_ref[...] = scaled
+        scaled_ref[...] = scaled.astype(jnp.float32)
         part = lax.dot_general(
             scaled, scaled, (((1,), (1,)), ((), ())), preferred_element_type=jnp.float32
         )
@@ -230,29 +230,44 @@
             landed(low.at[pl.ds(0, chips - 1)], 5)
 
         above = top[...].reshape(half, count)
-        below = jnp.concatenate([jnp.transpose(above[:, half:]), low[...].reshape(half, half)], axis=1)
-        g = jnp.concatenate([above, below], axis=0)
-        d_row, d_col = right_row, right_col
-        r_row, r_col = right_row, right_col
-        c_row, c_col = jnp.zeros_like(right_row), jnp.zeros_like(right_col)
-        rr = total_lanes(r_row * r_row)
+        g_aa, g_ab = above[:, :half], above[:, half:]
+        g_bb = low[...].reshape(half, half)
+        g_ba = jnp.transpose(g_ab)
+        cols = [right_col[:half], right_col[half:]]
+        rows_of = [right_row[:, :half], right_row[:, half:]]
+        d_row, r_row, d_col, r_col = rows_of, rows_of, cols, cols
+        c_row = [jnp.zeros_like(v) for v in rows_of]
+        c_col = [jnp.zeros_like(v) for v in cols]
+
+        def inner(u, v):
+            return total_lanes(u[0] * v[0] + u[1] * v[1])
+
+        rr = inner(r_row, r_row)
         for turn in range(ITERS):
-            image_row = total_rows(g * d_col) + SHIFT * d_row
-            size = rr / total_lanes(d_row * image_row)
-            c_row = c_row + size * d_row
-            c_col = c_col + size * d_col
+            image_row = [
+                total_rows(g_aa * d_col[0] + g_ba * d_col[1]) + SHIFT * d_row[0],
+                total_rows(g_ab * d_col[0] + g_bb * d_col[1]) + SHIFT * d_row[1],
+            ]
+            size = rr / inner(d_row, image_row)
+            c_row = [c + size * d for c, d in zip(c_row, d_row)]
+            c_col = [c + size * d for c, d in zip(c_col, d_col)]
             if turn == ITERS - 1:
                 break
-            image_col = total_lanes(g * d_row) + SHIFT * d_col
-            r_row = r_row - size * image_row
-            r_col = r_col - size * image_col
-            fresh = total_lanes(r_row * r_row)
+            image_col = [
+                total_lanes(g_aa * d_row[0] + g_ab * d_row[1]) + SHIFT * d_col[0],
+                total_lanes(g_ba * d_row[0] + g_bb * d_row[1]) + SHIFT * d_col[1],
+            ]
+            r_row = [r - size * v for r, v in zip(r_row, image_row)]
+            r_col = [r - size * v for r, v in zip(r_col, image_col)]
+            fresh = inner(r_row, r_row)
             ratio = fresh / rr
-            d_row = r_row + ratio * d_row
-            d_col = r_col + ratio * d_col
+            d_row = [r + ratio * d for r, d in zip(r_row, d_row)]
+            d_col = [r + ratio * d for r, d in zip(r_col, d_col)]
             rr = fresh
 
-        update[s] = total_rows(scaled_ref[...].astype(jnp.float32) * c_col)
+        c_row = jnp.concatenate(c_row, axis=1)
+
+        update[s] = total_rows(scaled_ref[:half] * c_col[0] + scaled_ref[half:] * c_col[1])
 
         def give_piece(there):
             remote(update.at[s], update.at[s], 6, (there, p)).start()
@@ -301,11 +316,11 @@
         pl.semaphore_wait(barrier, team)
         for there in team_ids:
             give_rows(there)
+        sent(jbuf.at[pl.ds(0, team)], 0)
         for there in team_ids:
             give_energies(there)
         landed(cbuf, 7)
         coeffs[...] = cbuf[...][0, :rows]
-        sent(jbuf.at[pl.ds(0, team)], 0)
         sent(ebuf.at[pl.ds(0, team)], 1)
         landed(update, 6)
 
@@ -376,7 +391,7 @@
                 pltpu.VMEM((samp, rows, width), jnp.float32),
                 pltpu.VMEM((samp, 1, LANES), jnp.float32),
                 pltpu.VMEM((1, LANES), jnp.float32),
-                pltpu.VMEM((count, width), jnp.bfloat16),
+                pltpu.VMEM((count, width), jnp.float32),
                 pltpu.VMEM((2 * chips, share, count), jnp.float32),
                 pltpu.VMEM((2 * chips, share, count), jnp.float32),
                 pltpu.VMEM((depth, share, count), jnp.float32),

time: 41.1 us -> 41 us (level)
  no operation moved by 1% of the time
where the time goes in v6:
time: 41 us; the launch traced here: 40.9 us
  Pallas kernels  40.2 us (98%)
  between operations  0.64 us (2%)
    pallas_call x1, Pallas kernels, per_device(): pl.pallas_call(functools.partial(kernel, samp, par), out_shape=(jax.Shape...  39.6 us

profile of v6, /device:TPU:1, one launch (start us, length us, event | category | flops | bytes accessed | tf_op | source)
XLA Modules:
  0.0 40.9 jit_solution(12325618355556983286)
XLA Ops:
  0.6 39.6 %shard_map.41 = (f32[16,1,512]{2,1,0:T(1,128)S(1)}, f32[8]{0:T(128)S(1)}) custom-call(f32[8,8192]{1,0:T(8,128)} %jac.1, f32[8]{0:T(128)} %energies.1), custom_call_target="tpu_custom_call" | custom-call | tf_op jit(solution)/shard_map/pallas_call | solution.py:374
  40.2 0.6 %shard_map.42 = (f32[8192]{0:T(1024)}, f32[8]{0:T(128)}) custom-call(f32[8192]{0:T(1024)S(1)} %bitcast.1, f32[8]{0:T(128)S(1)} %get-tuple-element.5.coeffs), custom_call_target="tpu_custom_call" | custom-call | tf_op jit(solution)/shard_map/pallas_call | solution.py:349

commit v7 on v6

--- a/solution.py
+++ b/solution.py
@@ -88,6 +88,8 @@
     z_steps = sorted(range(depth), key=lambda k: -away(k, depth))
     z_ids = [z_at[k] * CORES + core for k in z_steps[:-1]]
     team_ids = [z_at[k] * CORES + core_at[c] for k in z_steps for c in (1, 0)]
+    by_core_ids = [z_at[k] * CORES + core_at[c] for c in (1, 0) for k in z_steps]
+    fixed_core_ids = [z_at[k] * CORES + c for c in range(CORES) for k in z_steps]
     chip_steps = sorted(
         [(j, i) for j in range(Y_LO) for i in range(xs) if (j, i) != (0, 0)],
         key=lambda k: -k[0] - away(k[1], xs),
@@ -194,8 +196,8 @@
         def spread(part_of, mine_of, which):
             landed(ar.at[z_others, :, part_of], 3)
             mine_of[p] = jnp.sum(ar[:, :, part_of], axis=0)
-            for there in chip_ids:
-                for there_core in range(CORES):
+            for there_core in range(CORES):
+                for there in chip_ids:
                     remote(mine_of.at[p], mine_of.at[p], which, (at_core(there_core), there)).start()
             remote(mine_of.at[p], mine_of.at[p], which, (at_core(1 - core), p)).start()
 
@@ -314,7 +316,7 @@
     @pl.when(sender)
     def _():
         pl.semaphore_wait(barrier, team)
-        for there in team_ids:
+        for there in fixed_core_ids:
             give_rows(there)
         sent(jbuf.at[pl.ds(0, team)], 0)
         for there in team_ids:
@@ -327,7 +329,7 @@
     @pl.when(worker)
     def _():
         pl.semaphore_wait(barrier, team - 1 + par - 1)
-        for there in team_ids[:-1]:
+        for there in by_core_ids[:-1]:
             give_rows(there)
         ebuf[s] = mine
         jbuf[s] = jown[s]

time: 41 us -> 40 us (0.976)
  Pallas kernels: 40.2 us -> 39.2 us
    pallas_call x1, Pallas kernels: 39.6 us -> 38.6 us  [per_device(): pl.pallas_call(functools.partial(kernel, samp, par), out_shape=(jax.Shape...]
where the time goes in v7:
time: 40 us; the launch traced here: 39.9 us
  Pallas kernels  39.2 us (98%)
  between operations  0.64 us (2%)
    pallas_call x1, Pallas kernels, per_device(): pl.pallas_call(functools.partial(kernel, samp, par), out_shape=(jax.Shape...  38.6 us

profile of v7, /device:TPU:1, one launch (start us, length us, event | category | flops | bytes accessed | tf_op | source)
XLA Modules:
  0.0 39.9 jit_solution(9602775425385354717)
XLA Ops:
  0.6 38.6 %shard_map.41 = (f32[16,1,512]{2,1,0:T(1,128)S(1)}, f32[8]{0:T(128)S(1)}) custom-call(f32[8,8192]{1,0:T(8,128)} %jac.1, f32[8]{0:T(128)} %energies.1), custom_call_target="tpu_custom_call" | custom-call | tf_op jit(solution)/shard_map/pallas_call | solution.py:376
  39.2 0.6 %shard_map.42 = (f32[8192]{0:T(1024)}, f32[8]{0:T(128)}) custom-call(f32[8192]{0:T(1024)S(1)} %bitcast.1, f32[8]{0:T(128)S(1)} %get-tuple-element.5.coeffs), custom_call_target="tpu_custom_call" | custom-call | tf_op jit(solution)/shard_map/pallas_call | solution.py:351

commit v8 on v7

--- a/solution.py
+++ b/solution.py
@@ -329,8 +329,12 @@
     @pl.when(worker)
     def _():
         pl.semaphore_wait(barrier, team - 1 + par - 1)
-        for there in by_core_ids[:-1]:
-            give_rows(there)
+        for there in fixed_core_ids:
+
+            @pl.when(there != s)
+            def _(there=there):
+                give_rows(there)
+
         ebuf[s] = mine
         jbuf[s] = jown[s]
         landed(jbuf.at[pl.ds(0, samp - 1)], 0)

time: 40 us -> 40 us (level)
  no operation moved by 1% of the time
where the time goes in v8:
time: 40 us; the launch traced here: 39.9 us
  Pallas kernels  39.2 us (98%)
  between operations  0.64 us (2%)
    pallas_call x1, Pallas kernels, per_device(): pl.pallas_call(functools.partial(kernel, samp, par), out_shape=(jax.Shape...  38.6 us

profile of v8, /device:TPU:1, one launch (start us, length us, event | category | flops | bytes accessed | tf_op | source)
XLA Modules:
  0.0 39.9 jit_solution(2806957762781546498)
XLA Ops:
  0.6 38.6 %shard_map.41 = (f32[16,1,512]{2,1,0:T(1,128)S(1)}, f32[8]{0:T(128)S(1)}) custom-call(f32[8,8192]{1,0:T(8,128)} %jac.1, f32[8]{0:T(128)} %energies.1), custom_call_target="tpu_custom_call" | custom-call | tf_op jit(solution)/shard_map/pallas_call | solution.py:380
  39.2 0.6 %shard_map.42 = (f32[8192]{0:T(1024)}, f32[8]{0:T(128)}) custom-call(f32[8192]{0:T(1024)S(1)} %bitcast.1, f32[8]{0:T(128)S(1)} %get-tuple-element.5.coeffs), custom_call_target="tpu_custom_call" | custom-call | tf_op jit(solution)/shard_map/pallas_call | solution.py:355

commit v9 on v7

--- a/solution.py
+++ b/solution.py
@@ -274,10 +274,14 @@
         def give_piece(there):
             remote(update.at[s], update.at[s], 6, (there, p)).start()
 
-        for there in team_ids[:-1]:
-            give_piece(there)
+        for there in [z_at[k] * CORES + c for c in reversed(range(CORES)) for k in z_steps]:
+
+            @pl.when(there != s)
+            def _(there=there):
+                give_piece(there)
+
             give_piece(there + team)
-        give_piece(s + team)
+
 
         def own_samples(first):
             here = lax.rem(s, team) // per

time: 40 us -> 39.9 us (level)
  no operation moved by 1% of the time
where the time goes in v9:
time: 39.9 us; the launch traced here: 39.8 us
  Pallas kernels  39.1 us (98%)
  between operations  0.64 us (2%)
    pallas_call x1, Pallas kernels, per_device(): pl.pallas_call(functools.partial(kernel, samp, par), out_shape=(jax.Shape...  38.5 us

profile of v9, /device:TPU:1, one launch (start us, length us, event | category | flops | bytes accessed | tf_op | source)
XLA Modules:
  0.0 39.8 jit_solution(17277960999913843375)
XLA Ops:
  0.6 38.5 %shard_map.41 = (f32[16,1,512]{2,1,0:T(1,128)S(1)}, f32[8]{0:T(128)S(1)}) custom-call(f32[8,8192]{1,0:T(8,128)} %jac.1, f32[8]{0:T(128)} %energies.1), custom_call_target="tpu_custom_call" | custom-call | tf_op jit(solution)/shard_map/pallas_call | solution.py:380
  39.2 0.6 %shard_map.42 = (f32[8192]{0:T(1024)}, f32[8]{0:T(128)}) custom-call(f32[8192]{0:T(1024)S(1)} %bitcast.1, f32[8]{0:T(128)S(1)} %get-tuple-element.5.coeffs), custom_call_target="tpu_custom_call" | custom-call | tf_op jit(solution)/shard_map/pallas_call | solution.py:355

commit v10 on v9

--- a/solution.py
+++ b/solution.py
@@ -333,8 +333,12 @@
     @pl.when(worker)
     def _():
         pl.semaphore_wait(barrier, team - 1 + par - 1)
-        for there in by_core_ids[:-1]:
-            give_rows(there)
+        for there in fixed_core_ids:
+
+            @pl.when(there != s)
+            def _(there=there):
+                give_rows(there)
+
         ebuf[s] = mine
         jbuf[s] = jown[s]
         landed(jbuf.at[pl.ds(0, samp - 1)], 0)

time: 39.9 us -> 39.9 us (level)
  no operation moved by 1% of the time
where the time goes in v10:
time: 39.9 us; the launch traced here: 39.8 us
  Pallas kernels  39.1 us (98%)
  between operations  0.64 us (2%)
    pallas_call x1, Pallas kernels, per_device(): pl.pallas_call(functools.partial(kernel, samp, par), out_shape=(jax.Shape...  38.5 us

profile of v10, /device:TPU:1, one launch (start us, length us, event | category | flops | bytes accessed | tf_op | source)
XLA Modules:
  0.0 39.8 jit_solution(12774837502872287090)
XLA Ops:
  0.6 38.5 %shard_map.41 = (f32[16,1,512]{2,1,0:T(1,128)S(1)}, f32[8]{0:T(128)S(1)}) custom-call(f32[8,8192]{1,0:T(8,128)} %jac.1, f32[8]{0:T(128)} %energies.1), custom_call_target="tpu_custom_call" | custom-call | tf_op jit(solution)/shard_map/pallas_call | solution.py:384
  39.2 0.6 %shard_map.42 = (f32[8192]{0:T(1024)}, f32[8]{0:T(128)}) custom-call(f32[8192]{0:T(1024)S(1)} %bitcast.1, f32[8]{0:T(128)S(1)} %get-tuple-element.5.coeffs), custom_call_target="tpu_custom_call" | custom-call | tf_op jit(solution)/shard_map/pallas_call | solution.py:359
